TPU v7x, 256 devices: a whole 4x4x8 slice. The times are simulated.
256 devices in a mesh: stn: 64 (over z, y_hi, x), chan: 4 (over y_lo, core).
Axes of the slice: x: 4, y: 4 (y_hi: 2, y_lo: 2; y = y_hi * 2 + y_lo), z: 8, core: 2. Of those that a mesh axis runs over, the one named last changes fastest.
Arguments:
- samples: bfloat16 [512, 17, 2, 8192], P(('stn', 'chan')), may hold values from -6 to 6
- keeper: int32 [64, 64], replicated, may hold values from 0 to 1, as said below
Outputs:
- visibilities: bfloat16 [512, 2, 4096, 264], P('stn', None, 'chan')
Inputs may be any that keep to these rules, and one draw needn't show every extreme that they name: keeper[g, g] is 1; for g != h with d = (g - h) mod 64: keeper[g, h] is 1 where 0 < d < 32, 0 where d > 32, and at d = 32 exactly one of keeper[g, h] and keeper[h, g] is 1, which one drawn for each such pair; half of the rows hold 33 ones, the others 33 - 1.
All inputs are finite; a program needn't handle non-finite values.
Results may differ from a plain program's by a relative error of at most 0.0077.
Values may be sent and summed in bfloat16 or wider, within the bound.
No kernel may reach another device: no remote copies, remote signals or barrier semaphores. Data moves between devices by JAX's collectives and lax.ppermute only.
A program may use at most 192 MiB of HBM per device.

v0:
```python
import math
import jax
import jax.numpy as jnp
from jax import lax
from jax.sharding import PartitionSpec as P

NFFT = 8192
TAPS = 16
CH_WIN = 1024
DFT_BLOCK = 256


def taps_table():
    pos = jnp.arange(TAPS * NFFT).astype(jnp.float32)
    shifted = (pos + 0.5) / NFFT - TAPS / 2.0
    window = 0.5 - 0.5 * jnp.cos(2.0 * math.pi * (pos + 0.5) / (TAPS * NFFT))
    return (jnp.sinc(shifted) * window).reshape(TAPS, NFFT)


def twiddles(width):
    index_n = jnp.arange(NFFT, dtype=jnp.int32)[:, None]
    index_k = jnp.arange(width, dtype=jnp.int32)[None, :]
    phase = (index_n * index_k % NFFT).astype(jnp.float32) * (2.0 * math.pi / NFFT)
    cosines = jnp.cos(phase).astype(jnp.bfloat16)
    sines = jnp.sin(phase).astype(jnp.bfloat16)
    upper = jnp.concatenate([cosines, -sines], axis=1)
    lower = jnp.concatenate([sines, cosines], axis=1)
    return jnp.concatenate([upper, lower], axis=0)


def rotations(ch_tot, width):
    blocks = ch_tot // width
    index_n = jnp.arange(NFFT, dtype=jnp.int32)[None, :]
    index_b = jnp.arange(blocks, dtype=jnp.int32)[:, None]
    phase = (index_n * index_b * width % NFFT).astype(jnp.float32) * (2.0 * math.pi / NFFT)
    return (jnp.cos(phase), jnp.sin(phase))


def channelise(block, taps, table, cos_rot, sin_rot, ch_tot):
    frames = block.shape[1] - TAPS + 1
    count = block.shape[0]
    width = table.shape[1] // 2
    blocks = ch_tot // width
    total = taps[0] * block[:, 0:frames].astype(jnp.float32)
    for tap in range(1, TAPS):
        total = total + taps[tap] * block[:, tap : tap + frames].astype(jnp.float32)
    real_part = total[:, :, 0][None]
    imag_part = total[:, :, 1][None]
    cosine = cos_rot[:, None, None, :]
    sine = sin_rot[:, None, None, :]
    rot_real = real_part * cosine + imag_part * sine
    rot_imag = imag_part * cosine - real_part * sine
    lhs = jnp.stack([rot_real, rot_imag], axis=3).astype(jnp.bfloat16)
    lhs = lhs.reshape(blocks * count * frames, 2 * NFFT)
    spectrum = jnp.dot(lhs, table, preferred_element_type=jnp.float32) * (1.0 / math.sqrt(NFFT))
    spectrum = spectrum.astype(jnp.bfloat16).reshape(blocks, count, frames, 2, width)
    spectrum = jnp.transpose(spectrum, (1, 0, 4, 3, 2))
    return spectrum.reshape(count, ch_tot, 2, frames)


def correlate(own, others, frames):
    half = others.shape[2] // 2
    turned = jnp.concatenate([-others[:, :, half:], others[:, :, :half]], axis=2)
    rhs = jnp.concatenate([others, turned], axis=0)
    product = lax.dot_general(
        own, rhs, (((2,), (2,)), ((1,), (1,))), preferred_element_type=jnp.float32
    )
    rows = others.shape[0]
    product = product.reshape(product.shape[0], product.shape[1], 2, rows)
    return jnp.transpose(product, (1, 2, 0, 3)) / frames


def slot_table(keep_rows, keep_slots):
    ranking = jnp.cumsum(keep_rows, axis=1) - 1
    slot_index = jnp.arange(keep_slots, dtype=jnp.int32)
    matched = (keep_rows[:, :, None] == 1) & (ranking[:, :, None] == slot_index[None, None, :])
    column_ids = jnp.arange(keep_rows.shape[1], dtype=jnp.int32)
    slot_column = jnp.sum(jnp.where(matched, column_ids[None, :, None], 0), axis=1)
    filled = jnp.any(matched, axis=1)
    return (slot_column, filled)


def per_device(samples, keeper):
    n_chan = lax.axis_size("chan")
    n_stn = lax.axis_size("stn")
    ch_tot = CH_WIN * n_chan
    frames = samples.shape[1] - TAPS + 1
    cos_rot, sin_rot = rotations(ch_tot, DFT_BLOCK)
    spectrum = channelise(samples, taps_table(), twiddles(DFT_BLOCK), cos_rot, sin_rot, ch_tot)
    local = lax.all_to_all(spectrum, "chan", split_axis=1, concat_axis=0, tiled=True)
    group_in = local.shape[0]
    own = local.reshape(group_in, CH_WIN, 2 * frames)
    keep_slots = n_stn // 2 + 1
    group_index = lax.axis_index("stn")
    row_keep = jnp.take(keeper, group_index, axis=0)
    slot_column, filled = slot_table(row_keep[None], keep_slots)
    slot_column = slot_column[0]
    filled = filled[0]
    nothing = jnp.zeros((), jnp.bfloat16)
    col_mask = jnp.repeat(row_keep, group_in).astype(jnp.float32)
    tile = correlate(own, lax.all_gather(own, "stn", axis=0, tiled=True), frames)
    whole = (tile * col_mask[None, None, None, :]).astype(jnp.bfloat16)
    whole = whole.reshape(group_in, 2, CH_WIN, n_stn, group_in)
    picked = jnp.take(whole, slot_column, axis=3)
    picked = jnp.where(filled[None, None, None, :, None], picked, nothing)
    return picked.reshape(group_in, 2, CH_WIN, keep_slots * group_in)


def solution(mesh):
    placed = (P(("stn", "chan"), None, None, None), P())
    return jax.shard_map(
        per_device,
        mesh=mesh,
        in_specs=placed,
        out_specs=P("stn", None, "chan", None),
        check_vma=False,
    )
```

profile of v0, /device:TPU:2, one launch (start us, length us, event | category | flops | bytes accessed | tf_op | source)
XLA Modules:
  0.0 386.7 jit_solution(5526646558050877336)
XLA Ops:
  6.5 2.4 fusion.33
  8.9 2.1 fusion.45
  11.0 35.0 %sine_convert_fusion = (bf16[8192,256]{1,0:T(8,128)(2,1)}, bf16[8192,256]{1,0:T(8,128)(2,1)}) fusion(), kind=kLoop, calls=%fused_computation.25 | loop fusion | flops 33554432 | bytes 8388608 | tf_op jit(solution)/shard_map/convert_element_type | solution.py:25
  46.0 32.4 %fusion.22 = bf16[8192,256]{1,0:T(8,128)(2,1)} fusion(), kind=kLoop, calls=%fused_computation.34 | loop fusion | flops 37748736 | bytes 4194304 | tf_op jit(solution)/shard_map/neg | solution.py:26
  78.4 2.1 multiply_add_fusion.1
  81.0 4.4 %add_convert_fusion = (bf16[16,2,2,1,8192]{4,3,2,1,0:T(2,128)(2,1)S(1)}, bf16[16,2,2,1,8192]{4,3,2,1,0:T(2,128)(2,1)S(1)}) fusion(f32[16,8192]{1,0:T(8,128)S(1)} %get-tuple-element.42, f32[2,2,8192]{2,1,0:T(2,128)S(1)} %get-tuple-element.40, f32[16,8192]{1,0:T(8,128)S(1)} %get-tuple-element.43, f32[2,2,8192]{2,1,0:T(2,128)S(1)} %get-tuple-element.41), kind=kLoop, calls=%fused_computation.33 | loop fusion | flops 4194304 | bytes 3407872 | tf_op jit(solution)/shard_map/convert
  85.4 4.8 %pad_maximum_fusion = bf16[16,2,2,2,8192]{4,3,2,1,0:T(2,128)(2,1)S(1)} fusion(bf16[16,2,2,1,8192]{4,3,2,1,0:T(2,128)(2,1)S(1)} %get-tuple-element.21, bf16[16,2,2,1,8192]{4,3,2,1,0:T(2,128)(2,1)S(1)} %get-tuple-element.20), kind=kLoop, calls=%fused_computation.31 | loop fusion | flops 4194304 | bytes 4194304 | tf_op jit(solution)/shard_map/stack | solution.py:53
  90.2 1.2 copy.51
  91.4 13.7 %fusion.26 = bf16[64,512]{1,0:T(8,128)(2,1)S(1)} fusion(bf16[64,16384]{1,0:T(8,128)(2,1)S(1)} %bitcast.44, bf16[8192,256]{1,0:T(8,128)(2,1)} %get-tuple-element.45, bf16[8192,256]{1,0:T(8,128)(2,1)} %get-tuple-element.44, bf16[8192,256]{1,0:T(8,128)(2,1)} %fusion.22), kind=kOutput, calls=%fused_computation.36 | convolution fusion | flops 1140916224 | bytes 14745600 | tf_op jit(solution)/shard_map/dot_general | solution.py:55
  105.2 4.8 %copy.46 = bf16[2,16,256,2,2]{4,3,0,2,1:T(2,128)(2,1)} copy(bf16[2,16,256,2,2]{2,1,4,3,0:T(8,128)(2,1)S(1)} %bitcast.45) | data formatting | bytes 131072 | tf_op jit(solution)/shard_map/reshape | solution.py:58
  110.0 7.2 %reshape.361 = bf16[4,2,4096]{2,1,0:T(2,128)(2,1)S(1)} reshape(bf16[4096,2,2,2]{3,2,1,0:T(2,128)(2,1)} %bitcast.41) | data formatting | bytes 131072
  117.2 6.8 %all_to_all.15 = bf16[4,2,4096]{2,1,0:T(2,128)(2,1)S(1)} all-to-all(bf16[4,2,4096]{2,1,0:T(2,128)(2,1)S(1)} %reshape.361), channel_id=1, replica_groups=mesh['stn'=64,'chan'=4] {'chan'}, dimensions={0} | all-to-all | bytes 131072 | tf_op jit(solution)/shard_map/all_to_all | solution.py:90
  123.9 10.0 %reshape.362 = bf16[4096,2,2,2]{3,2,1,0:T(2,128)(2,1)} reshape(bf16[4,2,4096]{2,1,0:T(2,128)(2,1)S(1)} %all_to_all.15) | data formatting | bytes 131072
  133.9 9.7 %copy.47 = bf16[2,4,1024,2,2]{2,1,4,3,0:T(4,128)(2,1)S(1)} copy(bf16[2,4,1024,2,2]{4,3,0,2,1:T(2,128)(2,1)} %bitcast.42) | data formatting | bytes 131072 | tf_op jit(solution)/shard_map/all_to_all | solution.py:90
  145.7 0.7 select_reduce_fusion
  149.3 125.9 %all-gather.2.cloned.1.call-done = bf16[512,1024,4]{1,2,0:T(4,128)(2,1)} async-done(((bf16[8,1024,4]{1,2,0:T(4,128)(2,1)}), bf16[512,1024,4]{1,2,0:T(4,128)(2,1)}) %all-gather.2.cloned.1.call-update) | async-done | bytes 4194320 | tf_op jit(solution)/shard_map/all_gather | solution.py:101
  275.2 10.1 %copy.41 = bf16[512,1024,4]{0,2,1:T(4,128)(2,1)} copy(bf16[512,1024,4]{1,2,0:T(4,128)(2,1)} %all-gather.2.cloned.1.call-done) | data formatting | bytes 8388608 | tf_op jit(solution)/shard_map/all_gather | solution.py:101
  285.3 7.7 %slice_negate_fusion = (bf16[512,1024,2]{0,2,1:T(2,128)(2,1)S(1)}, bf16[512,1024,2]{0,2,1:T(2,128)(2,1)S(1)}) fusion(bf16[512,1024,4]{0,2,1:T(4,128)(2,1)} %copy.41), kind=kLoop, calls=%fused_computation.30 | loop fusion | flops 1048576 | bytes 8388608 | tf_op jit(solution)/shard_map/neg | solution.py:63
  293.1 13.0 %fusion.13 = f32[1024,8,1024]{2,1,0:T(8,128)} fusion(bf16[8,1024,4]{0,2,1:T(4,128)(2,1)S(1)} %copy.42, bf16[512,1024,2]{0,2,1:T(2,128)(2,1)S(1)} %get-tuple-element.19, bf16[512,1024,2]{0,2,1:T(2,128)(2,1)S(1)} %get-tuple-element.18, bf16[512,1024,4]{0,2,1:T(4,128)(2,1)S(1)} %copy-done), kind=kOutput, calls=%fused_computation.19 | convolution fusion | flops 92274688 | bytes 42008576 | tf_op jit(solution)/shard_map/dot_general | solution.py:65
  306.1 32.2 %copy.43 = f32[1024,8,2,512]{0,3,2,1:T(8,128)} copy(f32[1024,8,2,512]{3,1,2,0:T(8,128)} %bitcast.40) | data formatting | bytes 67108864 | tf_op jit(solution)/shard_map/reshape | solution.py:69
  338.3 13.4 %fusion = bf16[8,2,1024,64,8]{2,4,3,1,0:T(8,128)(2,1)S(1)} fusion(f32[1024,8,2,512]{0,3,2,1:T(8,128)} %copy.43, f32[512]{0:T(512)S(1)} %mul.838), kind=kLoop, calls=%fused_computation.2 | loop fusion | flops 16777216 | bytes 50333696 | tf_op jit(solution)/shard_map/reshape | solution.py:103
  351.7 7.0 %copy.44 = bf16[8,2,1024,64,8]{2,4,1,0,3:T(8,128)(2,1)} copy(bf16[8,2,1024,64,8]{2,4,3,1,0:T(8,128)(2,1)S(1)} %fusion) | data formatting | bytes 33554432 | tf_op jit(solution)/shard_map/reshape | solution.py:103
  358.7 10.9 %gather_fusion = bf16[33,8,2,1024,8]{3,4,2,1,0:T(8,128)(2,1)} fusion(bf16[8,2,1024,64,8]{2,4,1,0,3:T(8,128)(2,1)} %copy.44, s32[1024]{0:T(1024)S(1)} %pad_clamp_fusion), kind=kCustom, calls=%fused_computation | custom fusion | bytes 17301636 | tf_op jit(solution)/shard_map/jit(_take)/gather | solution.py:104
  369.6 10.3 %fusion.9 = bf16[8,2,1024,264]{2,3,1,0:T(8,128)(2,1)} fusion(pred[264]{0:T(512)(128)(4,1)S(1)} %copy-done.2, pred[264]{0:T(512)(128)(4,1)S(1)} %copy-done.3, bf16[33,8,2,1024,8]{3,4,2,1,0:T(8,128)(2,1)} %gather_fusion), kind=kLoop, calls=%fused_computation.15 | loop fusion | flops 8650752 | bytes 17302032 | tf_op jit(solution)/shard_map/jit(_where)/select_n | solution.py:105
  (34 shorter events, 5.4 us)
Async XLA Ops:
  6.5 71.9 %copy-start.1 = (bf16[2,17,2,8192]{3,2,1,0:T(2,128)(2,1)S(1)}, bf16[2,17,2,8192]{3,2,1,0:T(2,128)(2,1)}, u32[]{:S(2)}) copy-start(bf16[2,17,2,8192]{3,2,1,0:T(2,128)(2,1)} %param.2) | copy-start | bytes 3342340
  6.5 268.7 %all-gather.2.cloned.1.call-start = ((), (), s32[]{:S(2)}) async-start(), calls=%async_computation.1 | async-start | bytes 4259840 | tf_op jit(solution)/shard_map/all_gather | solution.py:101
  285.3 7.8 %copy-start = (bf16[512,1024,4]{0,2,1:T(4,128)(2,1)S(1)}, bf16[512,1024,4]{0,2,1:T(4,128)(2,1)}, u32[]{:S(2)}) copy-start(bf16[512,1024,4]{0,2,1:T(4,128)(2,1)} %copy.41) | copy-start | bytes 12582916
  358.7 10.9 %copy-start.2 = (pred[264]{0:T(512)(128)(4,1)S(1)}, pred[264]{0:T(512)(128)(4,1)}, u32[]{:S(2)}) copy-start(pred[264]{0:T(512)(128)(4,1)} %broadcast_in_dim.82) | copy-start | bytes 796
  358.7 10.9 %copy-start.3 = (pred[264]{0:T(512)(128)(4,1)S(1)}, pred[264]{0:T(512)(128)(4,1)}, u32[]{:S(2)}) copy-start(pred[264]{0:T(512)(128)(4,1)} %broadcast_in_dim.77) | copy-start | bytes 796
Sparse Core Ops, SparseCore 0:
  144.6 130.5 all-gather.1
where the time goes:
time: 388 us; the launch traced here: 387 us
  waiting for transfers between devices  126 us (32%)
  other arithmetic  117 us (30%)
  local copies, waits for them, and re-layouts  96.8 us (25%)
  matrix products  26.7 us (7%)
  between operations  13.6 us (4%)
  blocking collectives  6.77 us (2%)
    all_gather x1, waiting for transfers between devices, per_device(): lax.all_gather(own, 'stn', axis=0, tiled=True)  126 us
    convert_element_type x1, other arithmetic, twiddles(): sines = jnp.sin(phase).astype(jnp.bfloat16)  35 us
    neg x1, other arithmetic, twiddles(): upper = jnp.concatenate([cosines, -sines], axis=1)  32.4 us
    reshape x1, local copies, waits for them, and re-layouts, correlate(): product = product.reshape(product.shape[0], product.shape[1], 2, rows)  32.2 us
    unnamed x12, local copies, waits for them, and re-layouts  18.6 us
    dot_general x1, matrix products, channelise(): jnp.dot(lhs, table, preferred_element_type=jnp.float32)  13.7 us
    reshape x1, other arithmetic, per_device(): whole = whole.reshape(group_in, 2, CH_WIN, n_stn, group_in)  13.4 us
    dot_general x1, matrix products, correlate(): lax.dot_general(own, rhs, (((2,), (2,)), ((1,), (1,))), preferred_element...  13 us
  transfers between devices with their start and end apart: 1, of which 1 were waited for; matrix products, arithmetic and copies ran while one was open for 1% of the time, Pallas kernels for 0%

commit v1 on v0

--- a/solution.py
+++ b/solution.py
@@ -98,7 +98,13 @@
     filled = filled[0]
     nothing = jnp.zeros((), jnp.bfloat16)
     col_mask = jnp.repeat(row_keep, group_in).astype(jnp.float32)
-    tile = correlate(own, lax.all_gather(own, "stn", axis=0, tiled=True), frames)
+    tile = correlate(
+        own,
+        jnp.concatenate(
+            lax.all_to_all(jnp.stack([own] * lax.axis_size("stn")), "stn", 0, 0), axis=0
+        ),
+        frames,
+    )
     whole = (tile * col_mask[None, None, None, :]).astype(jnp.bfloat16)
     whole = whole.reshape(group_in, 2, CH_WIN, n_stn, group_in)
     picked = jnp.take(whole, slot_column, axis=3)

time: 388 us -> 358 us (0.923)
  waiting for transfers between devices: 126 us -> 89.6 us
  starting transfers between devices: 0.01 us -> 14.6 us
  between operations: 13.6 us -> 0.19 us
  local copies, waits for them, and re-layouts: 96.8 us -> 101 us
    all_gather x1 -> x0, waiting for transfers between devices: 126 us -> none  [per_device(): lax.all_gather(own, 'stn', axis=0, tiled=True)]
    all_to_all x0 -> x1, waiting for transfers between devices: none -> 89.6 us  [per_device(): lax.all_to_all(jnp.stack([own] * lax.axis_size('stn')), 'stn', 0, 0)]
    all_to_all x0 -> x1, starting transfers between devices: none -> 14.6 us  [per_device(): lax.all_to_all(jnp.stack([own] * lax.axis_size('stn')), 'stn', 0, 0)]
    all_gather x1 -> x0, local copies, waits for them, and re-layouts: 10.1 us -> none  [per_device(): lax.all_gather(own, 'stn', axis=0, tiled=True)]
    reshape x0 -> x1, local copies, waits for them, and re-layouts: none -> 7.84 us  [per_device(): jnp.concatenate(lax.all_to_all(jnp.stack([own] * lax.axis_size('stn')), '...]
    all_to_all x0 -> x1, local copies, waits for them, and re-layouts: none -> 4.79 us  [per_device(): lax.all_to_all(jnp.stack([own] * lax.axis_size('stn')), 'stn', 0, 0)]
where the time goes in v1:
time: 358 us; the launch traced here: 356 us
  other arithmetic  117 us (33%)
  local copies, waits for them, and re-layouts  101 us (28%)
  waiting for transfers between devices  89.6 us (25%)
  matrix products  26.7 us (7%)
  starting transfers between devices  14.6 us (4%)
  blocking collectives  6.77 us (2%)
    all_to_all x1, waiting for transfers between devices, per_device(): lax.all_to_all(jnp.stack([own] * lax.axis_size('stn')), 'stn', 0, 0)  89.6 us
    convert_element_type x1, other arithmetic, twiddles(): sines = jnp.sin(phase).astype(jnp.bfloat16)  35 us
    neg x1, other arithmetic, twiddles(): upper = jnp.concatenate([cosines, -sines], axis=1)  32.4 us
    reshape x1, local copies, waits for them, and re-layouts, correlate(): product = product.reshape(product.shape[0], product.shape[1], 2, rows)  32.2 us
    unnamed x12, local copies, waits for them, and re-layouts  18.6 us
    all_to_all x1, starting transfers between devices, per_device(): lax.all_to_all(jnp.stack([own] * lax.axis_size('stn')), 'stn', 0, 0)  14.6 us
    dot_general x1, matrix products, channelise(): jnp.dot(lhs, table, preferred_element_type=jnp.float32)  13.7 us
    reshape x1, other arithmetic, per_device(): whole = whole.reshape(group_in, 2, CH_WIN, n_stn, group_in)  13.4 us
  transfers between devices with their start and end apart: 1, of which 1 were waited for; matrix products, arithmetic and copies ran while one was open for 1% of the time, Pallas kernels for 0%

profile of v1, /device:TPU:2, one launch (start us, length us, event | category | flops | bytes accessed | tf_op | source)
XLA Modules:
  0.0 355.7 jit_solution(2182086236013867504)
XLA Ops:
  0.0 2.4 fusion.33
  4.5 35.0 %sine_convert_fusion = (bf16[8192,256]{1,0:T(8,128)(2,1)}, bf16[8192,256]{1,0:T(8,128)(2,1)}) fusion(), kind=kLoop, calls=%fused_computation.25 | loop fusion | flops 33554432 | bytes 8388608 | tf_op jit(solution)/shard_map/convert_element_type | solution.py:25
  39.5 32.4 %fusion.22 = bf16[8192,256]{1,0:T(8,128)(2,1)} fusion(), kind=kLoop, calls=%fused_computation.35 | loop fusion | flops 37748736 | bytes 4194304 | tf_op jit(solution)/shard_map/neg | solution.py:26
  71.9 2.1 multiply_add_fusion.1
  74.4 4.4 %add_convert_fusion = (bf16[16,2,2,1,8192]{4,3,2,1,0:T(2,128)(2,1)S(1)}, bf16[16,2,2,1,8192]{4,3,2,1,0:T(2,128)(2,1)S(1)}) fusion(f32[16,8192]{1,0:T(8,128)S(1)} %get-tuple-element.42, f32[2,2,8192]{2,1,0:T(2,128)S(1)} %get-tuple-element.40, f32[16,8192]{1,0:T(8,128)S(1)} %get-tuple-element.43, f32[2,2,8192]{2,1,0:T(2,128)S(1)} %get-tuple-element.41), kind=kLoop, calls=%fused_computation.34 | loop fusion | flops 4194304 | bytes 3407872 | tf_op jit(solution)/shard_map/convert
  78.8 4.8 %pad_maximum_fusion = bf16[16,2,2,2,8192]{4,3,2,1,0:T(2,128)(2,1)S(1)} fusion(bf16[16,2,2,1,8192]{4,3,2,1,0:T(2,128)(2,1)S(1)} %get-tuple-element.21, bf16[16,2,2,1,8192]{4,3,2,1,0:T(2,128)(2,1)S(1)} %get-tuple-element.20), kind=kLoop, calls=%fused_computation.32 | loop fusion | flops 4194304 | bytes 4194304 | tf_op jit(solution)/shard_map/stack | solution.py:53
  84.9 13.7 %fusion.26 = bf16[64,512]{1,0:T(8,128)(2,1)S(1)} fusion(bf16[64,16384]{1,0:T(8,128)(2,1)S(1)} %bitcast.48, bf16[8192,256]{1,0:T(8,128)(2,1)} %get-tuple-element.45, bf16[8192,256]{1,0:T(8,128)(2,1)} %get-tuple-element.44, bf16[8192,256]{1,0:T(8,128)(2,1)} %fusion.22), kind=kOutput, calls=%fused_computation.37 | convolution fusion | flops 1140916224 | bytes 14745600 | tf_op jit(solution)/shard_map/dot_general | solution.py:55
  98.6 4.8 %copy.50 = bf16[2,16,256,2,2]{4,3,0,2,1:T(2,128)(2,1)} copy(bf16[2,16,256,2,2]{2,1,4,3,0:T(8,128)(2,1)S(1)} %bitcast.49) | data formatting | bytes 131072 | tf_op jit(solution)/shard_map/reshape | solution.py:58
  103.4 7.2 %reshape.368 = bf16[4,2,4096]{2,1,0:T(2,128)(2,1)S(1)} reshape(bf16[4096,2,2,2]{3,2,1,0:T(2,128)(2,1)} %bitcast.44) | data formatting | bytes 131072
  110.6 6.8 %all_to_all.20 = bf16[4,2,4096]{2,1,0:T(2,128)(2,1)S(1)} all-to-all(bf16[4,2,4096]{2,1,0:T(2,128)(2,1)S(1)} %reshape.368), channel_id=1, replica_groups=mesh['stn'=64,'chan'=4] {'chan'}, dimensions={0} | all-to-all | bytes 131072 | tf_op jit(solution)/shard_map/all_to_all | solution.py:90
  117.4 10.0 %reshape.369 = bf16[4096,2,2,2]{3,2,1,0:T(2,128)(2,1)} reshape(bf16[4,2,4096]{2,1,0:T(2,128)(2,1)S(1)} %all_to_all.20) | data formatting | bytes 131072
  127.4 9.7 %copy.51 = bf16[2,4,1024,2,2]{2,1,4,3,0:T(4,128)(2,1)S(1)} copy(bf16[2,4,1024,2,2]{4,3,0,2,1:T(2,128)(2,1)} %bitcast.45) | data formatting | bytes 131072 | tf_op jit(solution)/shard_map/all_to_all | solution.py:90
  137.2 2.5 stack.10
  139.8 14.6 %all-to-all-start.1 = ((bf16[64,8,1024,4]{2,1,3,0:T(8,128)(2,1)}), bf16[64,8,1024,4]{2,1,3,0:T(8,128)(2,1)}, u32[]{:S(2)}, u32[]{:S(2)}) async-start(bf16[64,8,1024,4]{2,1,3,0:T(8,128)(2,1)} %stack.10), calls=%async_computation.1 | async-start | bytes 8388608 | tf_op jit(solution)/shard_map/all_to_all | solution.py:104
  159.1 89.6 %all-to-all-done.1 = bf16[64,8,1024,4]{2,1,3,0:T(8,128)(2,1)} async-done(((bf16[64,8,1024,4]{2,1,3,0:T(8,128)(2,1)}), bf16[64,8,1024,4]{2,1,3,0:T(8,128)(2,1)}, u32[]{:S(2)}, u32[]{:S(2)}) %all-to-all-start.1) | async-done | bytes 4194336 | tf_op jit(solution)/shard_map/all_to_all | solution.py:104
  248.7 4.8 %copy.61 = bf16[64,8,1024,4]{2,1,0,3:T(8,128)(2,1)} copy(bf16[64,8,1024,4]{2,1,3,0:T(8,128)(2,1)} %all-to-all-done.1) | data formatting | bytes 8388608 | tf_op jit(solution)/shard_map/all_to_all | solution.py:104
  253.5 7.8 %copy.45 = bf16[512,1024,4]{0,2,1:T(4,128)(2,1)} copy(bf16[512,1024,4]{1,0,2:T(8,128)(2,1)} %bitcast.46) | data formatting | bytes 8388608 | tf_op jit(solution)/shard_map/reshape | solution.py:103
  261.3 7.6 %slice_negate_fusion = (bf16[512,1024,2]{0,2,1:T(2,128)(2,1)S(1)}, bf16[512,1024,2]{0,2,1:T(2,128)(2,1)S(1)}) fusion(bf16[512,1024,4]{0,2,1:T(4,128)(2,1)} %copy.45), kind=kLoop, calls=%fused_computation.31 | loop fusion | flops 1048576 | bytes 8388608 | tf_op jit(solution)/shard_map/neg | solution.py:63
  268.9 13.0 %fusion.13 = f32[1024,8,1024]{2,1,0:T(8,128)} fusion(bf16[8,1024,4]{0,2,1:T(4,128)(2,1)S(1)} %copy.46, bf16[512,1024,2]{0,2,1:T(2,128)(2,1)S(1)} %get-tuple-element.19, bf16[512,1024,2]{0,2,1:T(2,128)(2,1)S(1)} %get-tuple-element.18, bf16[512,1024,4]{0,2,1:T(4,128)(2,1)S(1)} %copy-done), kind=kOutput, calls=%fused_computation.19 | convolution fusion | flops 92274688 | bytes 42008576 | tf_op jit(solution)/shard_map/dot_general | solution.py:65
  281.9 32.2 %copy.47 = f32[1024,8,2,512]{0,3,2,1:T(8,128)} copy(f32[1024,8,2,512]{3,1,2,0:T(8,128)} %bitcast.43) | data formatting | bytes 67108864 | tf_op jit(solution)/shard_map/reshape | solution.py:69
  314.1 13.4 %fusion = bf16[8,2,1024,64,8]{2,4,3,1,0:T(8,128)(2,1)S(1)} fusion(f32[1024,8,2,512]{0,3,2,1:T(8,128)} %copy.47, f32[512]{0:T(512)S(1)} %mul.838), kind=kLoop, calls=%fused_computation.2 | loop fusion | flops 16777216 | bytes 50333696 | tf_op jit(solution)/shard_map/reshape | solution.py:109
  327.5 7.0 %copy.48 = bf16[8,2,1024,64,8]{2,4,1,0,3:T(8,128)(2,1)} copy(bf16[8,2,1024,64,8]{2,4,3,1,0:T(8,128)(2,1)S(1)} %fusion) | data formatting | bytes 33554432 | tf_op jit(solution)/shard_map/reshape | solution.py:109
  334.5 10.9 %gather_fusion = bf16[33,8,2,1024,8]{3,4,2,1,0:T(8,128)(2,1)} fusion(bf16[8,2,1024,64,8]{2,4,1,0,3:T(8,128)(2,1)} %copy.48, s32[1024]{0:T(1024)S(1)} %pad_clamp_fusion), kind=kCustom, calls=%fused_computation | custom fusion | bytes 17301636 | tf_op jit(solution)/shard_map/jit(_take)/gather | solution.py:110
  345.4 10.3 %fusion.9 = bf16[8,2,1024,264]{2,3,1,0:T(8,128)(2,1)} fusion(pred[264]{0:T(512)(128)(4,1)S(1)} %copy-done.2, pred[264]{0:T(512)(128)(4,1)S(1)} %copy-done.3, bf16[33,8,2,1024,8]{3,4,2,1,0:T(8,128)(2,1)} %gather_fusion), kind=kLoop, calls=%fused_computation.15 | loop fusion | flops 8650752 | bytes 17302032 | tf_op jit(solution)/shard_map/jit(_where)/select_n | solution.py:111
  (34 shorter events, 8.5 us)
Async XLA Ops:
  0.0 71.9 %copy-start.1 = (bf16[2,17,2,8192]{3,2,1,0:T(2,128)(2,1)S(1)}, bf16[2,17,2,8192]{3,2,1,0:T(2,128)(2,1)}, u32[]{:S(2)}) copy-start(bf16[2,17,2,8192]{3,2,1,0:T(2,128)(2,1)} %param.2) | copy-start | bytes 3342340
  139.8 108.9 %all-to-all-start.1 = ((bf16[64,8,1024,4]{2,1,3,0:T(8,128)(2,1)}), bf16[64,8,1024,4]{2,1,3,0:T(8,128)(2,1)}, u32[]{:S(2)}, u32[]{:S(2)}) async-start(bf16[64,8,1024,4]{2,1,3,0:T(8,128)(2,1)} %stack.10), calls=%async_computation.1 | async-start | bytes 8388608 | tf_op jit(solution)/shard_map/all_to_all | solution.py:104
  261.3 7.6 %copy-start = (bf16[512,1024,4]{0,2,1:T(4,128)(2,1)S(1)}, bf16[512,1024,4]{0,2,1:T(4,128)(2,1)}, u32[]{:S(2)}) copy-start(bf16[512,1024,4]{0,2,1:T(4,128)(2,1)} %copy.45) | copy-start | bytes 12582916
  334.5 10.9 %copy-start.2 = (pred[264]{0:T(512)(128)(4,1)S(1)}, pred[264]{0:T(512)(128)(4,1)}, u32[]{:S(2)}) copy-start(pred[264]{0:T(512)(128)(4,1)} %broadcast_in_dim.82) | copy-start | bytes 796
  334.5 10.9 %copy-start.3 = (pred[264]{0:T(512)(128)(4,1)S(1)}, pred[264]{0:T(512)(128)(4,1)}, u32[]{:S(2)}) copy-start(pred[264]{0:T(512)(128)(4,1)} %broadcast_in_dim.77) | copy-start | bytes 796
